TPU v7x, 32 devices: a whole 2x2x4 slice. The times are simulated.
32 devices in a mesh: rep: 2 (over x), sp: 16 (over z, y, core).
Axes of the slice: x: 2, y: 2, z: 4, core: 2. Of those that a mesh axis runs over, the one named last changes fastest.
Arguments:
- volume: bfloat16 [128, 16, 16, 128], P(('rep', 'sp')), parts along dimension 0, may hold values from -6 to 6
- first_kernel: bfloat16 [3, 3, 3, 128, 128], replicated, may hold values from -0.15625 to 0.15625
- second_kernel: bfloat16 [3, 3, 3, 128, 256], replicated, may hold values from -0.15625 to 0.15625
- deep_kernel: bfloat16 [3, 3, 3, 256, 512], P(None, None, None, None, 'sp'), may hold values from -0.109375 to 0.109375
- deeper_kernel: bfloat16 [3, 3, 3, 512, 512], P(None, None, None, None, 'sp'), may hold values from -0.078125 to 0.078125
- rise_kernel: bfloat16 [2, 2, 2, 512, 256], replicated, may hold values from -0.375 to 0.375
- decode_kernel: bfloat16 [3, 3, 3, 512, 256], P(None, None, None, 'sp'), may hold values from -0.078125 to 0.078125
- final_kernel: bfloat16 [2, 2, 2, 256, 128], replicated, may hold values from -0.5 to 0.5
Outputs:
- segmented: bfloat16 [128, 16, 16, 128], P(('rep', 'sp')), parts along dimension 0
There are 2 independent parts, one for each index of `rep`. A program takes and returns all parts, laid end to end along the dimension named above; an argument that names none is the same for every part. Nothing has to cross between parts.
All inputs are finite; a program needn't handle non-finite values.
Results may differ from a plain program's by a relative error of at most 0.015.
Values may be sent and summed in bfloat16 or wider, within the bound.
No kernel may reach another device: no remote copies, remote signals or barrier semaphores. Data moves between devices by JAX's collectives and lax.ppermute only.
A program may use at most 64 MiB of HBM per device.

v0:
```python
import functools

import jax
import jax.numpy as jnp
import numpy as np
from jax import lax
from jax.experimental import pallas as pl
from jax.experimental.pallas import tpu as pltpu
from jax.sharding import PartitionSpec as P

GROUP = 4
MIB = 1024 * 1024


def call(kernel, outs, scratch, args, flops, vmem_mib, scalars=0):
    spaces = [pltpu.SMEM] * scalars + [pltpu.VMEM] * (len(args) - scalars)
    return pl.pallas_call(
        kernel,
        out_shape=outs,
        in_specs=[pl.BlockSpec(memory_space=space) for space in spaces],
        out_specs=jax.tree.map(lambda _: pl.BlockSpec(memory_space=pltpu.VMEM), outs),
        scratch_shapes=scratch,
        compiler_params=pltpu.CompilerParams(vmem_limit_bytes=vmem_mib * MIB),
        cost_estimate=pl.CostEstimate(
            flops=flops,
            bytes_accessed=sum(a.size * a.dtype.itemsize for a in args),
            transcendentals=0,
        ),
    )(*args)


def dot(left, right, dims=((1,), (0,))):
    return lax.dot_general(left, right, (dims, ((), ())), preferred_element_type=jnp.float32)


def round_once(values):
    return values.astype(jnp.bfloat16).astype(jnp.float32)


def fill_patches(framed, patches, slices):
    for b in range(3):
        for c in range(3):
            tap = framed[:, b : b + 8, 7 + c : 15 + c, :].reshape(slices * 64, 128)
            col = (b * 3 + c) * 128
            patches[:, col : col + 128] = tap.astype(jnp.bfloat16)


def stem_kernel(
    ends, low, volume, high, toeplitz, second, order,
    pooled_out, skip_out,
    shifted, halves, framed, patches, quarters,
):
    zero_row = jnp.zeros((16, 384), jnp.bfloat16)
    row = lax.broadcasted_iota(jnp.int32, (256, 128), 0) & 15
    for s in range(10):
        ref, at = (low, s) if s < 3 else (volume, s - 3) if s < 7 else (high, s - 7)
        here = ref[at].reshape(256, 128).astype(jnp.float32)
        before = jnp.where(row == 0, 0.0, pltpu.roll(here, 1, 0))
        after = jnp.where(row == 15, 0.0, pltpu.roll(here, 255, 0))
        shifted[s, 0] = zero_row
        shifted[s, 17] = zero_row
        for c, tap in enumerate((before, here, after)):
            shifted[s, 1:17, :, 128 * c : 128 * c + 128] = tap.astype(jnp.bfloat16).reshape(16, 16, 128)
    framed[...] = jnp.zeros(framed.shape, jnp.float32)
    for m in range(4):
        left = jnp.concatenate(
            [shifted[2 * m + j, b : b + 16].reshape(256, 384) for j in range(4) for b in range(3)],
            axis=1,
        )
        first = round_once(jnp.maximum(dot(left, toeplitz[...]), 0.0))
        pair = (first[:, :128] + first[:, 128:]).reshape(8, 32, 128)
        halves[...] = (pair[:, :16] + pair[:, 16:]).reshape(128, 128)
        pooled = halves[pl.ds(0, 64, stride=2), :] + halves[pl.ds(1, 64, stride=2), :]
        pooled = round_once(pooled * 0.125)
        if m == 0:
            pooled = jnp.where(ends[0] == 0, 0.0, pooled)
        if m == 3:
            pooled = jnp.where(ends[1] == 0, 0.0, pooled)
        framed[m, 1:9, 8:16, :] = pooled.reshape(8, 8, 128)
    fill_patches(framed, patches, 4)
    skip = dot(patches[0:128], second[0])
    skip += dot(patches[64:192], second[1])
    skip += dot(patches[128:256], second[2])
    skip = jnp.maximum(skip, 0.0).astype(jnp.bfloat16)
    wide = skip.astype(jnp.float32)
    pair = (wide[:64] + wide[64:]).reshape(4, 16, 256)
    pair = (pair[:, :8] + pair[:, 8:]).reshape(32, 256)
    for k in range(2):
        quarters[k] = pair[:, 128 * k : 128 * k + 128]
    pooled = jnp.concatenate(
        [
            quarters[k, pl.ds(0, 16, stride=2), :] + quarters[k, pl.ds(1, 16, stride=2), :]
            for k in range(2)
        ],
        axis=1,
    )
    pooled = (pooled * 0.125).astype(jnp.bfloat16)
    for dest in range(pooled_out.shape[0]):
        pooled_out[dest] = pooled
    sorted_skip = dot(skip, order[...])
    for r in range(GROUP):
        near, far = sorted_skip[:64, 64 * r : 64 * r + 64], sorted_skip[64:, 64 * r : 64 * r + 64]
        block = jnp.concatenate([near, far], axis=1).astype(jnp.bfloat16)
        for p in range(skip_out.shape[0] // GROUP):
            skip_out[GROUP * p + r] = block


def spread_taps(weights, values, dims, chans, voxels):
    lane = lax.broadcasted_iota(jnp.int32, (chans, voxels), 1)

    def moved(term, tap, step, place, last):
        if tap == 1:
            return term
        keep = place > 0 if tap == 0 else place < last
        return jnp.where(keep, pltpu.roll(term, ((1 - tap) * step) % voxels, 1), 0.0)

    total = None
    for a in range(3):
        products = dot(weights[a * 9 * chans : (a + 1) * 9 * chans, :], values, dims)
        plane = None
        for b in range(3):
            line = None
            for c in range(3):
                at = (b * 3 + c) * chans
                term = moved(products[at : at + chans], c, 1, lane & 3, 3)
                line = term if line is None else line + term
            line = moved(line, b, 4, (lane >> 2) & 3, 3)
            plane = line if plane is None else plane + line
        plane = moved(plane, a, 16, lane >> 4, voxels // 16 - 1)
        total = plane if total is None else total + plane
    return jnp.maximum(total, 0.0)


def deep_stage(pooled, weights, out):
    n, chans, voxels = out.shape
    deep = spread_taps(weights, pooled[...], ((1,), (1,)), chans, voxels).astype(jnp.bfloat16)
    for dest in range(n):
        out[dest] = deep


def deeper_stage(deep, weights, out):
    n, chans, _ = out.shape
    voxels = deep.shape[1]
    deeper = spread_taps(weights, deep[...], ((1,), (0,)), chans, voxels)
    lane = lax.broadcasted_iota(jnp.int32, (chans, 128), 1)
    planes = n // GROUP
    for p in range(planes):
        part = pltpu.roll(deeper, (16 - 64 * p) % voxels, 1)[:, :128]
        if p == 0:
            part = jnp.where(lane < 16, 0.0, part)
        if p == planes - 1:
            part = jnp.where(lane >= 80, 0.0, part)
        part = part.astype(jnp.bfloat16)
        for r in range(GROUP):
            out[GROUP * p + r] = part


def decode_stage(deeper, rise, skips, weights, out, framed, patches, risen):
    framed[...] = jnp.zeros(framed.shape, jnp.float32)
    spread = round_once(dot(deeper[...].astype(jnp.float32).T.astype(jnp.bfloat16), rise[...]))
    for pair in range(4):
        both = spread[:, 128 * pair : 128 * pair + 128]
        risen[2 * pair] = both
        risen[2 * pair + 1] = pltpu.roll(both, 64, 1)
    upper = lax.broadcasted_iota(jnp.int32, (64, 128), 1) >= 64
    for s in range(10):
        d, a = (s + 1) // 2, (s + 1) % 2
        for h in range(4):
            for b in range(2):
                for c in range(2):
                    framed[s, 1 + 2 * h + b, pl.ds(8 + c, 4, stride=2), :] = risen[
                        4 * a + 2 * b + c, 16 * d + 4 * h : 16 * d + 4 * h + 4, :
                    ]
        skip = skips[d].astype(jnp.float32)
        if a == 0:
            skip = pltpu.roll(skip, 64, 1)
        joined = framed[s, 1:9, 8:16, :].reshape(64, 128)
        framed[s, 1:9, 8:16, :] = jnp.where(upper, skip, joined).reshape(8, 8, 128)
    fill_patches(framed, patches, 10)
    partial = dot(patches[0:512], weights[0])
    partial += dot(patches[64:576], weights[1])
    partial += dot(patches[128:640], weights[2])
    out[...] = partial.astype(jnp.bfloat16)


def final_stage(partials, weights, out, spaced):
    decoded = partials[0].astype(jnp.float32)
    for g in range(1, GROUP):
        decoded += partials[g].astype(jnp.float32)
    decoded = jnp.maximum(decoded, 0.0).astype(jnp.bfloat16)
    for a in range(2):
        for b in range(2):
            for c in range(2):
                values = dot(decoded, weights[4 * a + 2 * b + c])
                for d in range(2):
                    for h in range(8):
                        at = ((2 * d + a) * 16 + 2 * h + b) * 16 + c
                        spaced[pl.ds(at, 8, stride=2), :] = values[64 * d + 8 * h : 64 * d + 8 * h + 8]
    out[...] = spaced[...].astype(jnp.bfloat16)


def exchange(payload, groups=None):
    return lax.all_to_all(
        payload, "sp", split_axis=0, concat_axis=0, tiled=True, axis_index_groups=groups
    )


def body(
    volume,
    first_kernel,
    second_kernel,
    deep_kernel,
    deeper_kernel,
    rise_kernel,
    decode_kernel,
    final_kernel,
):
    n = lax.axis_size("sp")
    place = lax.axis_index("sp")
    planes = n // GROUP
    plane, rank = place // GROUP, place % GROUP
    chans = deep_kernel.shape[4]
    voxels = 16 * n
    columns = [[r + GROUP * j for j in range(planes)] for r in range(GROUP)]
    rows = [[GROUP * p + r for r in range(GROUP)] for p in range(planes)]
    bf16 = functools.partial(jax.ShapeDtypeStruct, dtype=jnp.bfloat16)

    decode_part = lax.all_gather(
        decode_kernel, "sp", axis=3, tiled=True, axis_index_groups=columns
    ).reshape(3, 1152, 256)

    forward = [(i, i + 1) for i in range(n - 1)]
    backward = [(target, source) for source, target in forward]
    low = lax.ppermute(volume[1:], "sp", forward)
    high = lax.ppermute(volume[:3], "sp", backward)

    lane = np.arange(256)
    source = (lane // 64 + GROUP * (lane % 64 // chans)) * chans + lane % chans
    order = jnp.asarray(np.arange(256)[:, None] == source[None, :], jnp.bfloat16)
    taps = first_kernel.reshape(3, 1152, 128)
    none = jnp.zeros((1, 1152, 128), jnp.bfloat16)
    toeplitz = jnp.concatenate(
        [jnp.concatenate([taps, none], axis=0), jnp.concatenate([none, taps], axis=0)], axis=2
    ).reshape(4608, 256)
    ends = jnp.stack([place, n - 1 - place]).astype(jnp.int32)
    pooled_two, sends = call(
        stem_kernel,
        (bf16((n, 16, 256)), bf16((n, 64, 128))),
        [
            pltpu.VMEM((10, 18, 16, 384), jnp.bfloat16),
            pltpu.VMEM((128, 128), jnp.float32),
            pltpu.VMEM((4, 10, 24, 128), jnp.float32),
            pltpu.VMEM((256, 1152), jnp.bfloat16),
            pltpu.VMEM((2, 32, 128), jnp.float32),
        ],
        (ends, low, volume, high, toeplitz, second_kernel.reshape(3, 1152, 256), order),
        2 * 1024 * 4608 * 256,
        24,
        scalars=1,
    )
    pooled_whole = exchange(pooled_two)
    skips = exchange(sends)

    deep = call(
        deep_stage,
        bf16((n, chans, voxels)),
        [],
        (
            pooled_whole.reshape(voxels, 256),
            deep_kernel.transpose(0, 1, 2, 4, 3).reshape(27 * chans, 256),
        ),
        2 * 27 * chans * 256 * voxels,
        16,
    )
    deep_whole = exchange(deep).reshape(n * chans, voxels)

    deeper = call(
        deeper_stage,
        bf16((n, chans, 128)),
        [],
        (deep_whole, deeper_kernel.transpose(0, 1, 2, 4, 3).reshape(27 * chans, n * chans)),
        2 * 27 * chans * n * chans * voxels,
        16,
    )
    deeper_near = exchange(deeper).reshape(n * chans, 128)

    mine = lax.dynamic_slice_in_dim(order, 64 * rank, 64, axis=1)
    rise_part = jnp.einsum("pio,os->ips", rise_kernel.reshape(8, n * chans, 256), mine)
    rise_part = rise_part.reshape(n * chans, 512)
    skips = jnp.pad(skips, ((1, 1), (0, 0), (0, 0)))
    skips = lax.dynamic_slice_in_dim(skips, GROUP * plane, GROUP + 2, axis=0)
    partial = call(
        decode_stage,
        bf16((512, 256)),
        [
            pltpu.VMEM((10, 10, 24, 128), jnp.float32),
            pltpu.VMEM((640, 1152), jnp.bfloat16),
            pltpu.VMEM((8, 128, 128), jnp.float32),
        ],
        (deeper_near, rise_part, skips, decode_part),
        2 * 512 * 3456 * 256,
        24,
    )
    partials = exchange(partial.reshape(GROUP, 128, 256), rows)
    out = call(
        final_stage,
        bf16((1024, 128)),
        [pltpu.VMEM((1024, 128), jnp.float32)],
        (partials, final_kernel.reshape(8, 256, 128)),
        2 * 128 * 256 * 1024,
        16,
    )
    return out.reshape(4, 16, 16, 128)


def solution(mesh):
    return jax.shard_map(
        body,
        mesh=mesh,
        in_specs=(
            P(("rep", "sp"), None, None, None),
            P(),
            P(),
            P(None, None, None, None, "sp"),
            P(None, None, None, None, "sp"),
            P(),
            P(None, None, None, "sp", None),
            P(),
        ),
        out_specs=P(("rep", "sp"), None, None, None),
        check_vma=False,
    )
```

profile of v0, /device:TPU:1, one launch (start us, length us, event | category | flops | bytes accessed | tf_op | source)
XLA Modules:
  0.0 103.8 jit_solution(87837413300726989)
XLA Ops:
  6.5 0.0 copy-start
  6.5 0.0 all-gather.2.cloned.1.call-start
  6.5 0.7 all-gather.2.cloned.1.call-update
  7.3 1.1 %fusion.7 = (bf16[3,16,16,128]{3,2,1,0:T(8,128)(2,1)S(1)}, bf16[3,16,16,128]{3,2,1,0:T(8,128)(2,1)S(1)}) fusion(bf16[4,16,16,128]{3,2,1,0:T(8,128)(2,1)} %volume.1), kind=kLoop, calls=%fused_computation.11 | loop fusion | bytes 786432 | tf_op jit(solution)/shard_map/slice | solution.py:235
  8.4 4.5 %collective-permute-start = (bf16[3,16,16,128]{3,2,1,0:T(8,128)(2,1)S(1)}, bf16[3,16,16,128]{3,2,1,0:T(8,128)(2,1)S(1)}, u32[]{:S(2)}, u32[]{:S(2)}) collective-permute-start(bf16[3,16,16,128]{3,2,1,0:T(8,128)(2,1)S(1)} %get-tuple-element.10), channel_id=1, source_target_pairs={{0,1},{1,2},{2,3},{3,4},{4,5},{5,6},{6,7},{7,8},{8,9},{9,10},{10,1... | collective-permute-start | bytes 589832 | tf_op jit(solution)/shard_map/ppermute | solution.py:234
  12.9 1.9 %collective-permute-start.1 = (bf16[3,16,16,128]{3,2,1,0:T(8,128)(2,1)S(1)}, bf16[3,16,16,128]{3,2,1,0:T(8,128)(2,1)S(1)}, u32[]{:S(2)}, u32[]{:S(2)}) collective-permute-start(bf16[3,16,16,128]{3,2,1,0:T(8,128)(2,1)S(1)} %get-tuple-element.9), channel_id=1, source_target_pairs={{1,0},{2,1},{3,2},{4,3},{5,4},{6,5},{7,6},{8,7},{9,8},{10,9},{11,1... | collective-permute-start | bytes 589832 | tf_op jit(solution)/shard_map/ppermute | solution.py:235
  14.8 3.1 %fusion.2 = bf16[4,1152,256]{2,1,0:T(8,128)(2,1)} fusion(bf16[3,1152,128]{2,1,0:T(8,128)(2,1)} %bitcast.38), kind=kLoop, calls=%fused_computation.4 | loop fusion | flops 9437184 | bytes 3244032 | tf_op jit(solution)/shard_map/concatenate | solution.py:242
  17.9 0.1 pad_add_fusion.ends
  18.0 0.0 collective-permute-done.low
  18.0 1.9 %collective-permute-done.1.high = bf16[3,16,16,128]{3,2,1,0:T(8,128)(2,1)S(1)} collective-permute-done((bf16[3,16,16,128]{3,2,1,0:T(8,128)(2,1)S(1)}, bf16[3,16,16,128]{3,2,1,0:T(8,128)(2,1)S(1)}, u32[]{:S(2)}, u32[]{:S(2)}) %collective-permute-start.1) | collective-permute-done | bytes 196640 | tf_op jit(solution)/shard_map/ppermute | solution.py:235
  19.9 0.0 copy-done.6
  19.9 0.0 copy-done.3
  19.9 1.7 %copy-done.1 = bf16[4,1152,256]{2,1,0:T(8,128)(2,1)S(1)} copy-done((bf16[4,1152,256]{2,1,0:T(8,128)(2,1)S(1)}, bf16[4,1152,256]{2,1,0:T(8,128)(2,1)}, u32[]{:S(2)}) %copy-start.1) | copy-done | bytes 2359320
  21.6 1.5 %copy-done.7 = bf16[3,3,3,128,256]{4,3,2,1,0:T(8,128)(2,1)S(1)} copy-done((bf16[3,3,3,128,256]{4,3,2,1,0:T(8,128)(2,1)S(1)}, bf16[3,3,3,128,256]{4,3,2,1,0:T(8,128)(2,1)}, u32[]{:S(2)}) %copy-start.7) | copy-done | bytes 1769496
  23.0 4.8 %shard_map.91 = (bf16[16,16,256]{2,1,0:T(8,128)(2,1)S(1)}, bf16[16,64,128]{2,1,0:T(8,128)(2,1)}) custom-call(s32[2]{0:T(128)S(1)} %pad_add_fusion.ends, bf16[3,16,16,128]{3,2,1,0:T(8,128)(2,1)S(1)} %collective-permute-done.low, bf16[4,16,16,128]{3,2,1,0:T(8,128)(2,1)S(1)} %copy-done.3, bf16[3,16,16,128]{3,2,1,0:T(8,128)(2,1)S(1)} %collective-permute-done.1.high, ...), custom_call_target="tpu_custom_call" | custom-call | flops 2415919104 | bytes 4915208 | tf_op jit(solution)/shard_map/pallas_call | solution.py:17
  27.8 15.5 %all_to_all.25 = bf16[16,16,256]{2,1,0:T(8,128)(2,1)S(1)} all-to-all(bf16[16,16,256]{2,1,0:T(8,128)(2,1)S(1)} %get-tuple-element.7), channel_id=1, replica_groups=mesh['rep'=2,'sp'=16] {'sp'}, dimensions={0} | all-to-all | bytes 262144 | tf_op jit(solution)/shard_map/all_to_all | solution.py:203
  43.3 0.0 copy-done.5
  43.3 0.6 shard_map.92
  43.9 15.6 %all_to_all.26 = bf16[16,32,256]{2,1,0:T(8,128)(2,1)S(1)} all-to-all(bf16[16,32,256]{2,1,0:T(8,128)(2,1)S(1)} %shard_map.92), channel_id=1, replica_groups=mesh['rep'=2,'sp'=16] {'sp'}, dimensions={0} | all-to-all | bytes 524288 | tf_op jit(solution)/shard_map/all_to_all | solution.py:203
  59.4 4.3 %all-to-all-start.3 = ((bf16[16,64,128]{2,1,0:T(8,128)(2,1)}), bf16[16,64,128]{2,1,0:T(8,128)(2,1)}, u32[]{:S(2)}, u32[]{:S(2)}) async-start(bf16[16,64,128]{2,1,0:T(8,128)(2,1)} %get-tuple-element.8), calls=%async_computation.3 | async-start | bytes 524288 | tf_op jit(solution)/shard_map/all_to_all | solution.py:203
  63.8 1.3 %shard_map.93 = bf16[16,32,128]{2,1,0:T(8,128)(2,1)} custom-call(bf16[512,256]{1,0:T(8,128)(2,1)S(1)} %bitcast.28, bf16[864,512]{1,0:T(8,128)(2,1)S(1)} %bitcast.29), custom_call_target="tpu_custom_call" | custom-call | flops 226492416 | bytes 1146880 | tf_op jit(solution)/shard_map/pallas_call | solution.py:17
  65.1 8.3 %all-to-all-done.3 = bf16[16,64,128]{2,1,0:T(8,128)(2,1)} async-done(((bf16[16,64,128]{2,1,0:T(8,128)(2,1)}), bf16[16,64,128]{2,1,0:T(8,128)(2,1)}, u32[]{:S(2)}, u32[]{:S(2)}) %all-to-all-start.3) | async-done | bytes 262176 | tf_op jit(solution)/shard_map/all_to_all | solution.py:203
  73.4 4.0 %all-to-all-start.2 = ((bf16[16,32,128]{2,1,0:T(8,128)(2,1)}), bf16[16,32,128]{2,1,0:T(8,128)(2,1)S(1)}, u32[]{:S(2)}, u32[]{:S(2)}) async-start(bf16[16,32,128]{2,1,0:T(8,128)(2,1)} %shard_map.93), calls=%async_computation.2 | async-start | bytes 262144 | tf_op jit(solution)/shard_map/all_to_all | solution.py:203
  77.4 0.8 fusion.3
  78.2 0.2 copy.13.rise
  78.5 0.0 copy-start.4
  78.5 1.0 pad_dynamic-slice_fusion.skips
  79.4 4.9 %all-to-all-done.2 = bf16[16,32,128]{2,1,0:T(8,128)(2,1)S(1)} async-done(((bf16[16,32,128]{2,1,0:T(8,128)(2,1)}), bf16[16,32,128]{2,1,0:T(8,128)(2,1)S(1)}, u32[]{:S(2)}, u32[]{:S(2)}) %all-to-all-start.2) | async-done | bytes 131104 | tf_op jit(solution)/shard_map/all_to_all | solution.py:203
  84.3 1.5 %copy-done.8 = bf16[3,3,3,128,256]{4,3,2,1,0:T(8,128)(2,1)S(1)} copy-done((bf16[3,3,3,128,256]{4,3,2,1,0:T(8,128)(2,1)S(1)}, bf16[3,3,3,128,256]{4,3,2,1,0:T(8,128)(2,1)}, u32[]{:S(2)}) %copy-start.8) | copy-done | bytes 1769496
  85.8 1.5 %shard_map.94 = bf16[512,256]{1,0:T(8,128)(2,1)S(1)} custom-call(bf16[512,128]{1,0:T(8,128)(2,1)S(1)} %bitcast.34, bf16[512,512]{1,0:T(8,128)(2,1)S(1)} %copy.13.rise, bf16[6,64,128]{2,1,0:T(8,128)(2,1)S(1)} %pad_dynamic-slice_fusion.skips, bf16[3,1152,256]{2,1,0:T(8,128)(2,1)S(1)} %bitcast.36), custom_call_target="tpu_custom_call" | custom-call | flops 905969664 | bytes 2523136 | tf_op jit(solution)/shard_map/pallas_call | solution.py:17
  87.4 8.6 %all_to_all.27.partials = bf16[4,128,256]{2,1,0:T(8,128)(2,1)S(1)} all-to-all(bf16[4,128,256]{2,1,0:T(8,128)(2,1)S(1)} %bitcast.33), channel_id=1, replica_groups={{0,1,2,3},{4,5,6,7},{8,9,10,11},{12,13,14,15},{16,17,18,19},{20,21,22,2..., dimensions={0} | all-to-all | bytes 524288 | tf_op jit(solution)/shard_map/all_to_all | solution.py:203
  95.9 1.1 %shard_map.95 = bf16[1024,128]{1,0:T(8,128)(2,1)} custom-call(bf16[4,128,256]{2,1,0:T(8,128)(2,1)S(1)} %all_to_all.27.partials, bf16[8,256,128]{2,1,0:T(8,128)(2,1)S(1)} %bitcast.31), custom_call_target="tpu_custom_call" | custom-call | flops 67108864 | bytes 786432 | tf_op jit(solution)/shard_map/pallas_call | solution.py:17
  (11 shorter events, 0.0 us)
Async XLA Ops:
  6.5 70.8 %copy-start = (bf16[2,2,2,512,256]{4,3,2,1,0:T(8,128)(2,1)S(1)}, bf16[2,2,2,512,256]{4,3,2,1,0:T(8,128)(2,1)}, u32[]{:S(2)}) copy-start(bf16[2,2,2,512,256]{4,3,2,1,0:T(8,128)(2,1)} %param.14) | copy-start | bytes 6291460
  6.5 13.4 %copy-start.6 = (bf16[256,256]{1,0:T(8,128)(2,1)S(1)}, bf16[256,256]{1,0:T(8,128)(2,1)}, u32[]{:S(2)}) copy-start(bf16[256,256]{1,0:T(8,128)(2,1)} %constant.44.clone.order) | copy-start | bytes 393220
  6.5 13.4 %copy-start.3 = (bf16[4,16,16,128]{3,2,1,0:T(8,128)(2,1)S(1)}, bf16[4,16,16,128]{3,2,1,0:T(8,128)(2,1)}, u32[]{:S(2)}) copy-start(bf16[4,16,16,128]{3,2,1,0:T(8,128)(2,1)} %volume.1) | copy-start | bytes 786436
  6.5 77.8 %all-gather.2.cloned.1.call-start = ((), (), s32[]{:S(2)}) async-start(), calls=%async_computation.5 | async-start | bytes 2211840 | tf_op jit(solution)/shard_map/all_gather | solution.py:228
  8.4 9.6 %collective-permute-start = (bf16[3,16,16,128]{3,2,1,0:T(8,128)(2,1)S(1)}, bf16[3,16,16,128]{3,2,1,0:T(8,128)(2,1)S(1)}, u32[]{:S(2)}, u32[]{:S(2)}) collective-permute-start(bf16[3,16,16,128]{3,2,1,0:T(8,128)(2,1)S(1)} %get-tuple-element.10), channel_id=1, source_target_pairs={{0,1},{1,2},{2,3},{3,4},{4,5},{5,6},{6,7},{7,8},{8,9},{9,10},{10,1... | collective-permute-start | bytes 589832 | tf_op jit(solution)/shard_map/ppermute | solution.py:234
  12.9 7.0 %collective-permute-start.1 = (bf16[3,16,16,128]{3,2,1,0:T(8,128)(2,1)S(1)}, bf16[3,16,16,128]{3,2,1,0:T(8,128)(2,1)S(1)}, u32[]{:S(2)}, u32[]{:S(2)}) collective-permute-start(bf16[3,16,16,128]{3,2,1,0:T(8,128)(2,1)S(1)} %get-tuple-element.9), channel_id=1, source_target_pairs={{1,0},{2,1},{3,2},{4,3},{5,4},{6,5},{7,6},{8,7},{9,8},{10,9},{11,1... | collective-permute-start | bytes 589832 | tf_op jit(solution)/shard_map/ppermute | solution.py:235
  19.9 1.7 %copy-start.1 = (bf16[4,1152,256]{2,1,0:T(8,128)(2,1)S(1)}, bf16[4,1152,256]{2,1,0:T(8,128)(2,1)}, u32[]{:S(2)}) copy-start(bf16[4,1152,256]{2,1,0:T(8,128)(2,1)} %fusion.2) | copy-start | bytes 7077892
  21.6 1.5 %copy-start.7 = (bf16[3,3,3,128,256]{4,3,2,1,0:T(8,128)(2,1)S(1)}, bf16[3,3,3,128,256]{4,3,2,1,0:T(8,128)(2,1)}, u32[]{:S(2)}) copy-start(bf16[3,3,3,128,256]{4,3,2,1,0:T(8,128)(2,1)} %param.11) | copy-start | bytes 5308420
  23.0 20.2 %copy-start.5 = (bf16[3,3,3,256,32]{3,4,2,1,0:T(8,128)(2,1)S(1)}, bf16[3,3,3,256,32]{3,4,2,1,0:T(8,128)(2,1)}, u32[]{:S(2)}) copy-start(bf16[3,3,3,256,32]{3,4,2,1,0:T(8,128)(2,1)} %param.12) | copy-start | bytes 1327108
  27.8 35.9 %copy-start.2 = (bf16[3,3,3,512,32]{3,4,2,1,0:T(8,128)(2,1)S(1)}, bf16[3,3,3,512,32]{3,4,2,1,0:T(8,128)(2,1)}, u32[]{:S(2)}) copy-start(bf16[3,3,3,512,32]{3,4,2,1,0:T(8,128)(2,1)} %param.13) | copy-start | bytes 2654212
  59.4 14.0 %all-to-all-start.3 = ((bf16[16,64,128]{2,1,0:T(8,128)(2,1)}), bf16[16,64,128]{2,1,0:T(8,128)(2,1)}, u32[]{:S(2)}, u32[]{:S(2)}) async-start(bf16[16,64,128]{2,1,0:T(8,128)(2,1)} %get-tuple-element.8), calls=%async_computation.3 | async-start | bytes 524288 | tf_op jit(solution)/shard_map/all_to_all | solution.py:203
  73.4 10.9 %all-to-all-start.2 = ((bf16[16,32,128]{2,1,0:T(8,128)(2,1)}), bf16[16,32,128]{2,1,0:T(8,128)(2,1)S(1)}, u32[]{:S(2)}, u32[]{:S(2)}) async-start(bf16[16,32,128]{2,1,0:T(8,128)(2,1)} %shard_map.93), calls=%async_computation.2 | async-start | bytes 262144 | tf_op jit(solution)/shard_map/all_to_all | solution.py:203
  78.5 17.5 %copy-start.4 = (bf16[2,2,2,256,128]{4,3,2,1,0:T(8,128)(2,1)S(1)}, bf16[2,2,2,256,128]{4,3,2,1,0:T(8,128)(2,1)}, u32[]{:S(2)}) copy-start(bf16[2,2,2,256,128]{4,3,2,1,0:T(8,128)(2,1)} %param.16) | copy-start | bytes 1572868
  84.3 1.5 %copy-start.8 = (bf16[3,3,3,128,256]{4,3,2,1,0:T(8,128)(2,1)S(1)}, bf16[3,3,3,128,256]{4,3,2,1,0:T(8,128)(2,1)}, u32[]{:S(2)}) copy-start(bf16[3,3,3,128,256]{4,3,2,1,0:T(8,128)(2,1)} %all-gather.2.cloned.1.call-done) | copy-start | bytes 5308420
Sparse Core Ops, SparseCore 0:
  8.9 48.9 all-gather.1
where the time goes:
time: 105 us; the launch traced here: 104 us
  blocking collectives  39.6 us (38%)
  waiting for transfers between devices  15.8 us (15%)
  starting transfers between devices  14.7 us (14%)
  between operations  13.5 us (13%)
  Pallas kernels  9.28 us (9%)
  local copies, waits for them, and re-layouts  6.91 us (7%)
  other arithmetic  3.16 us (3%)
    all_to_all x3, blocking collectives, exchange(): lax.all_to_all(payload, 'sp', split_axis=0, concat_axis=0, tiled=True, ax...  39.6 us
    all_to_all x2, waiting for transfers between devices, exchange(): lax.all_to_all(payload, 'sp', split_axis=0, concat_axis=0, tiled=True, ax...  13.2 us
    pallas_call x5, Pallas kernels, call(): pl.pallas_call(kernel, out_shape=outs, in_specs=[pl.BlockSpec(memory_spac...  9.28 us
    all_to_all x2, starting transfers between devices, exchange(): lax.all_to_all(payload, 'sp', split_axis=0, concat_axis=0, tiled=True, ax...  8.29 us
    unnamed x18, local copies, waits for them, and re-layouts  4.64 us
    ppermute x1, starting transfers between devices, body(): low = lax.ppermute(volume[1:], 'sp', forward)  4.54 us
    concatenate x1, other arithmetic, body(): jnp.concatenate([jnp.concatenate([taps, none], axis=0), jnp.concatenate([...  3.08 us
  transfers between devices with their start and end apart: 5, of which 3 were waited for; matrix products, arithmetic and copies ran while one was open for 6% of the time, Pallas kernels for 6%

commit v1 on v0

--- a/solution.py
+++ b/solution.py
@@ -12,8 +12,11 @@
 MIB = 1024 * 1024
 
 
-def call(kernel, outs, scratch, args, flops, vmem_mib, scalars=0):
-    spaces = [pltpu.SMEM] * scalars + [pltpu.VMEM] * (len(args) - scalars)
+def call(kernel, outs, scratch, args, flops, vmem_mib, scalars=0, far=()):
+    spaces = [
+        pltpu.SMEM if i < scalars else pltpu.HBM if i in far else pltpu.VMEM
+        for i in range(len(args))
+    ]
     return pl.pallas_call(
         kernel,
         out_shape=outs,
@@ -45,29 +48,67 @@
             patches[:, col : col + 128] = tap.astype(jnp.bfloat16)
 
 
-def stem_kernel(
-    ends, low, volume, high, toeplitz, second, order,
-    pooled_out, skip_out,
-    shifted, halves, framed, patches, quarters,
+def shift_slice(shifted, s, values):
+    row = lax.broadcasted_iota(jnp.int32, (256, 128), 0) & 15
+    here = values.reshape(256, 128).astype(jnp.float32)
+    before = jnp.where(row == 0, 0.0, pltpu.roll(here, 1, 0))
+    after = jnp.where(row == 15, 0.0, pltpu.roll(here, 255, 0))
+    shifted[s, 0] = jnp.zeros((16, 384), jnp.bfloat16)
+    shifted[s, 17] = jnp.zeros((16, 384), jnp.bfloat16)
+    for c, tap in enumerate((before, here, after)):
+        tap = tap.astype(jnp.bfloat16).reshape(16, 16, 128)
+        shifted[s, 1:17, :, 128 * c : 128 * c + 128] = tap
+
+
+def depth_pair(shifted, slices, weights, steps):
+    left = jnp.concatenate(
+        [shifted[s, b : b + 16].reshape(256, 384) for s in slices for b in range(3)], axis=1
+    )
+    none = jnp.zeros((1152, 128), jnp.bfloat16)
+    right = [
+        jnp.concatenate(
+            [weights[j] if j < 3 else none, weights[j - 1] if j > 0 else none], axis=1
+        )
+        for j in steps
+    ]
+    return dot(left, jnp.concatenate(right, axis=0))
+
+
+def depth_one(shifted, s, weights):
+    left = jnp.concatenate([shifted[s, b : b + 16].reshape(256, 384) for b in range(3)], axis=1)
+    return dot(left, weights)
+
+
+def own_stage(volume, weights, out, shifted):
+    for s in range(4):
+        shift_slice(shifted, s, volume[s])
+    out[0, :, :128] = jnp.zeros((256, 128), jnp.float32)
+    out[0, :, 128:] = depth_one(shifted, 0, weights[2])
+    out[1] = depth_pair(shifted, (0, 1, 2), weights, (1, 2, 3))
+    out[2] = depth_pair(shifted, (1, 2, 3), weights, (0, 1, 2))
+    out[3, :, :128] = depth_one(shifted, 3, weights[0])
+    out[3, :, 128:] = jnp.zeros((256, 128), jnp.float32)
+
+
+def stem_stage(
+    ends, low, high, own, weights, second, order, out, shifted, halves, framed, patches, quarters
 ):
-    zero_row = jnp.zeros((16, 384), jnp.bfloat16)
-    row = lax.broadcasted_iota(jnp.int32, (256, 128), 0) & 15
-    for s in range(10):
-        ref, at = (low, s) if s < 3 else (volume, s - 3) if s < 7 else (high, s - 7)
-        here = ref[at].reshape(256, 128).astype(jnp.float32)
-        before = jnp.where(row == 0, 0.0, pltpu.roll(here, 1, 0))
-        after = jnp.where(row == 15, 0.0, pltpu.roll(here, 255, 0))
-        shifted[s, 0] = zero_row
-        shifted[s, 17] = zero_row
-        for c, tap in enumerate((before, here, after)):
-            shifted[s, 1:17, :, 128 * c : 128 * c + 128] = tap.astype(jnp.bfloat16).reshape(16, 16, 128)
+    for s in range(3):
+        shift_slice(shifted, s, low[s])
+        shift_slice(shifted, 3 + s, high[s])
     framed[...] = jnp.zeros(framed.shape, jnp.float32)
     for m in range(4):
-        left = jnp.concatenate(
-            [shifted[2 * m + j, b : b + 16].reshape(256, 384) for j in range(4) for b in range(3)],
-            axis=1,
-        )
-        first = round_once(jnp.maximum(dot(left, toeplitz[...]), 0.0))
+        if m == 0:
+            first = own[0] + depth_pair(shifted, (0, 1, 2), weights, (0, 1, 2))
+        elif m == 3:
+            first = own[3] + depth_pair(shifted, (3, 4, 5), weights, (1, 2, 3))
+        elif m == 1:
+            near = own[1, :, :128] + depth_one(shifted, 2, weights[0])
+            first = jnp.concatenate([near, own[1, :, 128:]], axis=1)
+        else:
+            far = own[2, :, 128:] + depth_one(shifted, 3, weights[2])
+            first = jnp.concatenate([own[2, :, :128], far], axis=1)
+        first = round_once(jnp.maximum(first, 0.0))
         pair = (first[:, :128] + first[:, 128:]).reshape(8, 32, 128)
         halves[...] = (pair[:, :16] + pair[:, 16:]).reshape(128, 128)
         pooled = halves[pl.ds(0, 64, stride=2), :] + halves[pl.ds(1, 64, stride=2), :]
@@ -95,14 +136,37 @@
         axis=1,
     )
     pooled = (pooled * 0.125).astype(jnp.bfloat16)
-    for dest in range(pooled_out.shape[0]):
-        pooled_out[dest] = pooled
     sorted_skip = dot(skip, order[...])
     for r in range(GROUP):
         near, far = sorted_skip[:64, 64 * r : 64 * r + 64], sorted_skip[64:, 64 * r : 64 * r + 64]
-        block = jnp.concatenate([near, far], axis=1).astype(jnp.bfloat16)
-        for p in range(skip_out.shape[0] // GROUP):
-            skip_out[GROUP * p + r] = block
+        block = jnp.concatenate([near, far], axis=1)
+        block = jnp.concatenate([block[:32], block[32:]], axis=1).astype(jnp.bfloat16)
+        out[r, 0:16, :] = pooled
+        out[r, 16:48, :] = block
+
+
+def relay_stage(plane, near, out):
+    lower = lax.broadcasted_iota(jnp.int32, (16, 128), 1) < 64
+
+    def edge(block, far):
+        sides = []
+        for k in range(2):
+            half = block[:, 128 * k : 128 * k + 128]
+            top, bottom = half[:16], half[16:]
+            if far:
+                top = pltpu.roll(top, 64, 1)
+            else:
+                bottom = pltpu.roll(bottom, 64, 1)
+            sides.append(jnp.where(lower, top, bottom))
+        return jnp.concatenate(sides, axis=1)
+
+    first = edge(near[0, 16:48, :].astype(jnp.float32), False)
+    last = edge(near[GROUP - 1, 16:48, :].astype(jnp.float32), True)
+    pooled = [near[r, 0:16, :] for r in range(GROUP)]
+    for p in range(out.shape[0]):
+        for r in range(GROUP):
+            out[p, 16 * r : 16 * r + 16, :] = pooled[r]
+        out[p, 64:80, :] = jnp.where(plane[0] < p, last, first).astype(jnp.bfloat16)
 
 
 def spread_taps(weights, values, dims, chans, voxels):
@@ -133,7 +197,8 @@
 
 def deep_stage(pooled, weights, out):
     n, chans, voxels = out.shape
-    deep = spread_taps(weights, pooled[...], ((1,), (1,)), chans, voxels).astype(jnp.bfloat16)
+    values = jnp.concatenate([pooled[p, 0:64, :] for p in range(n // GROUP)], axis=0)
+    deep = spread_taps(weights, values, ((1,), (1,)), chans, voxels).astype(jnp.bfloat16)
     for dest in range(n):
         out[dest] = deep
 
@@ -155,7 +220,13 @@
             out[GROUP * p + r] = part
 
 
-def decode_stage(deeper, rise, skips, weights, out, framed, patches, risen):
+def decode_stage(
+    plane, deeper, rise, near, relayed, decode, out, framed, patches, risen, weights, arrived
+):
+    copies = [pltpu.make_async_copy(decode.at[a], weights.at[a], arrived.at[a]) for a in range(3)]
+    for copy in copies:
+        copy.start()
+    planes = relayed.shape[0]
     framed[...] = jnp.zeros(framed.shape, jnp.float32)
     spread = round_once(dot(deeper[...].astype(jnp.float32).T.astype(jnp.bfloat16), rise[...]))
     for pair in range(4):
@@ -171,15 +242,28 @@
                     framed[s, 1 + 2 * h + b, pl.ds(8 + c, 4, stride=2), :] = risen[
                         4 * a + 2 * b + c, 16 * d + 4 * h : 16 * d + 4 * h + 4, :
                     ]
-        skip = skips[d].astype(jnp.float32)
-        if a == 0:
-            skip = pltpu.roll(skip, 64, 1)
+        if s == 0 or s == 9:
+            other = jnp.maximum(plane[0] - 1, 0) if s == 0 else jnp.minimum(plane[0] + 1, planes - 1)
+            edge = relayed[other, 64:80, :].astype(jnp.float32)
+            edge = jnp.where(other == plane[0], 0.0, edge)
+            parts = []
+            for k in range(2):
+                half = edge[:, 128 * k : 128 * k + 128]
+                parts += [pltpu.roll(half, 64, 1), half]
+            skip = jnp.concatenate(parts, axis=0)
+        else:
+            both = near[(s - 1) // 2, 16:48, :].astype(jnp.float32)
+            skip = jnp.concatenate([both[:, :128], both[:, 128:]], axis=0)
+            if (s - 1) % 2 == 0:
+                skip = pltpu.roll(skip, 64, 1)
         joined = framed[s, 1:9, 8:16, :].reshape(64, 128)
         framed[s, 1:9, 8:16, :] = jnp.where(upper, skip, joined).reshape(8, 8, 128)
     fill_patches(framed, patches, 10)
-    partial = dot(patches[0:512], weights[0])
-    partial += dot(patches[64:576], weights[1])
-    partial += dot(patches[128:640], weights[2])
+    partial = None
+    for a in range(3):
+        copies[a].wait()
+        term = dot(patches[64 * a : 64 * a + 512], weights[a])
+        partial = term if partial is None else partial + term
     out[...] = partial.astype(jnp.bfloat16)
 
 
@@ -234,41 +318,46 @@
     low = lax.ppermute(volume[1:], "sp", forward)
     high = lax.ppermute(volume[:3], "sp", backward)
 
+    taps = first_kernel.reshape(3, 1152, 128)
+    own = call(
+        own_stage,
+        jax.ShapeDtypeStruct((4, 256, 256), jnp.float32),
+        [pltpu.VMEM((4, 18, 16, 384), jnp.bfloat16)],
+        (volume, taps),
+        2 * 1024 * 2304 * 256,
+        24,
+    )
     lane = np.arange(256)
     source = (lane // 64 + GROUP * (lane % 64 // chans)) * chans + lane % chans
     order = jnp.asarray(np.arange(256)[:, None] == source[None, :], jnp.bfloat16)
-    taps = first_kernel.reshape(3, 1152, 128)
-    none = jnp.zeros((1, 1152, 128), jnp.bfloat16)
-    toeplitz = jnp.concatenate(
-        [jnp.concatenate([taps, none], axis=0), jnp.concatenate([none, taps], axis=0)], axis=2
-    ).reshape(4608, 256)
     ends = jnp.stack([place, n - 1 - place]).astype(jnp.int32)
-    pooled_two, sends = call(
-        stem_kernel,
-        (bf16((n, 16, 256)), bf16((n, 64, 128))),
+    sends = call(
+        stem_stage,
+        bf16((GROUP, 48, 256)),
         [
-            pltpu.VMEM((10, 18, 16, 384), jnp.bfloat16),
+            pltpu.VMEM((6, 18, 16, 384), jnp.bfloat16),
             pltpu.VMEM((128, 128), jnp.float32),
             pltpu.VMEM((4, 10, 24, 128), jnp.float32),
             pltpu.VMEM((256, 1152), jnp.bfloat16),
             pltpu.VMEM((2, 32, 128), jnp.float32),
         ],
-        (ends, low, volume, high, toeplitz, second_kernel.reshape(3, 1152, 256), order),
-        2 * 1024 * 4608 * 256,
+        (ends, low, high, own, taps, second_kernel.reshape(3, 1152, 256), order),
+        2 * 1024 * 2304 * 256,
         24,
         scalars=1,
     )
-    pooled_whole = exchange(pooled_two)
-    skips = exchange(sends)
+    near = exchange(sends, rows)
+    plane_ref = plane.astype(jnp.int32).reshape(1)
+    relays = call(
+        relay_stage, bf16((planes, 80, 256)), [], (plane_ref, near), 0, 16, scalars=1
+    )
+    relayed = exchange(relays, columns)
 
     deep = call(
         deep_stage,
         bf16((n, chans, voxels)),
         [],
-        (
-            pooled_whole.reshape(voxels, 256),
-            deep_kernel.transpose(0, 1, 2, 4, 3).reshape(27 * chans, 256),
-        ),
+        (relayed, deep_kernel.transpose(0, 1, 2, 4, 3).reshape(27 * chans, 256)),
         2 * 27 * chans * 256 * voxels,
         16,
     )
@@ -287,8 +376,6 @@
     mine = lax.dynamic_slice_in_dim(order, 64 * rank, 64, axis=1)
     rise_part = jnp.einsum("pio,os->ips", rise_kernel.reshape(8, n * chans, 256), mine)
     rise_part = rise_part.reshape(n * chans, 512)
-    skips = jnp.pad(skips, ((1, 1), (0, 0), (0, 0)))
-    skips = lax.dynamic_slice_in_dim(skips, GROUP * plane, GROUP + 2, axis=0)
     partial = call(
         decode_stage,
         bf16((512, 256)),
@@ -296,10 +383,14 @@
             pltpu.VMEM((10, 10, 24, 128), jnp.float32),
             pltpu.VMEM((640, 1152), jnp.bfloat16),
             pltpu.VMEM((8, 128, 128), jnp.float32),
+            pltpu.VMEM((3, 1152, 256), jnp.bfloat16),
+            pltpu.SemaphoreType.DMA((3,)),
         ],
-        (deeper_near, rise_part, skips, decode_part),
+        (plane_ref, deeper_near, rise_part, near, relayed, decode_part),
         2 * 512 * 3456 * 256,
         24,
+        scalars=1,
+        far=(5,),
     )
     partials = exchange(partial.reshape(GROUP, 128, 256), rows)
     out = call(

time: 105 us -> 100 us (0.952)
  blocking collectives: 39.6 us -> 24 us
  starting transfers between devices: 14.7 us -> 19.9 us
  waiting for transfers between devices: 15.8 us -> 20.7 us
  Pallas kernels: 9.28 us -> 12.7 us
  other arithmetic: 3.16 us -> 0.08 us
    all_to_all x3 -> x2, blocking collectives: 39.6 us -> 24 us  [exchange(): lax.all_to_all(payload, 'sp', split_axis=0, concat_axis=0, tiled=True, ax...]
    all_to_all x2 -> x3, waiting for transfers between devices: 13.2 us -> 18.6 us  [exchange(): lax.all_to_all(payload, 'sp', split_axis=0, concat_axis=0, tiled=True, ax...]
    all_to_all x2 -> x3, starting transfers between devices: 8.29 us -> 13.5 us  [exchange(): lax.all_to_all(payload, 'sp', split_axis=0, concat_axis=0, tiled=True, ax...]
    pallas_call x5 -> x7, Pallas kernels: 9.28 us -> 12.7 us  [call(): pl.pallas_call(kernel, out_shape=outs, in_specs=[pl.BlockSpec(memory_spac...]
    concatenate x1 -> x0, other arithmetic: 3.08 us -> none  [body(): jnp.concatenate([jnp.concatenate([taps, none], axis=0), jnp.concatenate([...]
    unnamed x18 -> x20, local copies, waits for them, and re-layouts: 4.64 us -> 4.63 us
  transfers between devices with their start and end apart: 5 -> 6, of which waited for: 3 -> 4; matrix products, arithmetic and copies ran while one was open for 6% -> 3% of each run, Pallas kernels for 6% -> 8%
where the time goes in v1:
time: 100 us; the launch traced here: 98.5 us
  blocking collectives  24 us (24%)
  waiting for transfers between devices  20.7 us (21%)
  starting transfers between devices  19.9 us (20%)
  between operations  13.5 us (14%)
  Pallas kernels  12.7 us (13%)
  local copies, waits for them, and re-layouts  5.89 us (6%)
  matrix products  1.67 us (2%)
    all_to_all x2, blocking collectives, exchange(): lax.all_to_all(payload, 'sp', split_axis=0, concat_axis=0, tiled=True, ax...  24 us
    all_to_all x3, waiting for transfers between devices, exchange(): lax.all_to_all(payload, 'sp', split_axis=0, concat_axis=0, tiled=True, ax...  18.6 us
    all_to_all x3, starting transfers between devices, exchange(): lax.all_to_all(payload, 'sp', split_axis=0, concat_axis=0, tiled=True, ax...  13.5 us
    pallas_call x7, Pallas kernels, call(): pl.pallas_call(kernel, out_shape=outs, in_specs=[pl.BlockSpec(memory_spac...  12.7 us
    unnamed x20, local copies, waits for them, and re-layouts  4.63 us
    ppermute x1, starting transfers between devices, body(): low = lax.ppermute(volume[1:], 'sp', forward)  4.55 us
  transfers between devices with their start and end apart: 6, of which 4 were waited for; matrix products, arithmetic and copies ran while one was open for 3% of the time, Pallas kernels for 8%

profile of v1, /device:TPU:1, one launch (start us, length us, event | category | flops | bytes accessed | tf_op | source)
XLA Modules:
  0.0 98.5 jit_solution(11455030143511950433)
XLA Ops:
  6.5 0.0 copy-start
  6.5 0.0 all-gather.2.cloned.1.call-start
  6.5 0.7 all-gather.2.cloned.1.call-update
  7.3 1.1 %fusion.4 = (bf16[3,16,16,128]{3,2,1,0:T(8,128)(2,1)S(1)}, bf16[3,16,16,128]{3,2,1,0:T(8,128)(2,1)S(1)}) fusion(bf16[4,16,16,128]{3,2,1,0:T(8,128)(2,1)} %volume.1), kind=kLoop, calls=%fused_computation.5 | loop fusion | bytes 786432 | tf_op jit(solution)/shard_map/slice | solution.py:319
  8.3 4.6 %collective-permute-start = (bf16[3,16,16,128]{3,2,1,0:T(8,128)(2,1)S(1)}, bf16[3,16,16,128]{3,2,1,0:T(8,128)(2,1)S(1)}, u32[]{:S(2)}, u32[]{:S(2)}) collective-permute-start(bf16[3,16,16,128]{3,2,1,0:T(8,128)(2,1)S(1)} %get-tuple-element.6), channel_id=1, source_target_pairs={{0,1},{1,2},{2,3},{3,4},{4,5},{5,6},{6,7},{7,8},{8,9},{9,10},{10,1... | collective-permute-start | bytes 589832 | tf_op jit(solution)/shard_map/ppermute | solution.py:318
  12.9 1.9 %collective-permute-start.1 = (bf16[3,16,16,128]{3,2,1,0:T(8,128)(2,1)S(1)}, bf16[3,16,16,128]{3,2,1,0:T(8,128)(2,1)S(1)}, u32[]{:S(2)}, u32[]{:S(2)}) collective-permute-start(bf16[3,16,16,128]{3,2,1,0:T(8,128)(2,1)S(1)} %get-tuple-element.5), channel_id=1, source_target_pairs={{1,0},{2,1},{3,2},{4,3},{5,4},{6,5},{7,6},{8,7},{9,8},{10,9},{11,1... | collective-permute-start | bytes 589832 | tf_op jit(solution)/shard_map/ppermute | solution.py:319
  14.8 0.1 pad_add_fusion.ends
  14.9 0.9 copy-done.2
  15.8 1.2 %copy-done.8 = bf16[3,3,3,128,128]{4,3,2,1,0:T(8,128)(2,1)S(1)} copy-done((bf16[3,3,3,128,128]{4,3,2,1,0:T(8,128)(2,1)S(1)}, bf16[3,3,3,128,128]{4,3,2,1,0:T(8,128)(2,1)}, u32[]{:S(2)}) %copy-start.8) | copy-done | bytes 884760
  17.0 1.4 %shard_map.91.own = f32[4,256,256]{2,1,0:T(8,128)S(1)} custom-call(bf16[4,16,16,128]{3,2,1,0:T(8,128)(2,1)S(1)} %copy-done.2, bf16[3,1152,128]{2,1,0:T(8,128)(2,1)S(1)} %bitcast.33), custom_call_target="tpu_custom_call" | custom-call | flops 1207959552 | bytes 1146880 | tf_op jit(solution)/shard_map/pallas_call | solution.py:20
  18.4 0.0 collective-permute-done.low
  18.4 1.4 %collective-permute-done.1.high = bf16[3,16,16,128]{3,2,1,0:T(8,128)(2,1)S(1)} collective-permute-done((bf16[3,16,16,128]{3,2,1,0:T(8,128)(2,1)S(1)}, bf16[3,16,16,128]{3,2,1,0:T(8,128)(2,1)S(1)}, u32[]{:S(2)}, u32[]{:S(2)}) %collective-permute-start.1) | collective-permute-done | bytes 196640 | tf_op jit(solution)/shard_map/ppermute | solution.py:319
  19.9 0.0 copy-done.5
  19.9 3.5 %shard_map.92 = bf16[4,48,256]{2,1,0:T(8,128)(2,1)} custom-call(s32[2]{0:T(128)S(1)} %pad_add_fusion.ends, bf16[3,16,16,128]{3,2,1,0:T(8,128)(2,1)S(1)} %collective-permute-done.low, bf16[3,16,16,128]{3,2,1,0:T(8,128)(2,1)S(1)} %collective-permute-done.1.high, f32[4,256,256]{2,1,0:T(8,128)S(1)} %shard_map.91.own, bf16[3,1152,128]{2,1,0:T(8,128)(2,1)S(1)} %bitcast.34, ...), custom_call_target="tpu_custom_call" | custom-call | flops 1207959552 | bytes 4227080 | tf_op jit(solution)/shard_map/pallas_call | solution.py:20
  23.4 3.9 %all-to-all-start = ((bf16[4,48,256]{2,1,0:T(8,128)(2,1)}), bf16[4,48,256]{2,1,0:T(8,128)(2,1)S(1)}, u32[]{:S(2)}, u32[]{:S(2)}) async-start(bf16[4,48,256]{2,1,0:T(8,128)(2,1)} %shard_map.92), calls=%async_computation | async-start | bytes 196608 | tf_op jit(solution)/shard_map/all_to_all | solution.py:287
  27.3 4.0 %all-to-all-done.near = bf16[4,48,256]{2,1,0:T(8,128)(2,1)S(1)} async-done(((bf16[4,48,256]{2,1,0:T(8,128)(2,1)}), bf16[4,48,256]{2,1,0:T(8,128)(2,1)S(1)}, u32[]{:S(2)}, u32[]{:S(2)}) %all-to-all-start) | async-done | bytes 98336 | tf_op jit(solution)/shard_map/all_to_all | solution.py:287
  31.3 0.1 shard_map.93
  31.4 15.5 %all_to_all.25.pooled.relayed = bf16[4,80,256]{2,1,0:T(8,128)(2,1)S(1)} all-to-all(bf16[4,80,256]{2,1,0:T(8,128)(2,1)S(1)} %shard_map.93), channel_id=1, replica_groups={{0,4,8,12},{1,5,9,13},{2,6,10,14},{3,7,11,15},{16,20,24,28},{17,21,25,2..., dimensions={0} | all-to-all | bytes 327680 | tf_op jit(solution)/shard_map/all_to_all | solution.py:287
  46.8 1.0 %copy-done.4 = bf16[3,3,3,256,32]{3,4,2,1,0:T(8,128)(2,1)S(1)} copy-done((bf16[3,3,3,256,32]{3,4,2,1,0:T(8,128)(2,1)S(1)}, bf16[3,3,3,256,32]{3,4,2,1,0:T(8,128)(2,1)}, u32[]{:S(2)}) %copy-start.4) | copy-done | bytes 442392
  47.8 1.3 %shard_map.94 = bf16[16,32,256]{2,1,0:T(8,128)(2,1)} custom-call(bf16[4,80,256]{2,1,0:T(8,128)(2,1)S(1)} %all_to_all.25.pooled.relayed, bf16[864,256]{1,0:T(8,128)(2,1)S(1)} %bitcast.29), custom_call_target="tpu_custom_call" | custom-call | flops 113246208 | bytes 606208 | tf_op jit(solution)/shard_map/pallas_call | solution.py:20
  49.1 5.0 %all-to-all-start.2 = ((bf16[16,32,256]{2,1,0:T(8,128)(2,1)}), bf16[16,32,256]{2,1,0:T(8,128)(2,1)S(1)}, u32[]{:S(2)}, u32[]{:S(2)}) async-start(bf16[16,32,256]{2,1,0:T(8,128)(2,1)} %shard_map.94), calls=%async_computation.2 | async-start | bytes 524288 | tf_op jit(solution)/shard_map/all_to_all | solution.py:287
  54.1 9.5 %all-to-all-done.2 = bf16[16,32,256]{2,1,0:T(8,128)(2,1)S(1)} async-done(((bf16[16,32,256]{2,1,0:T(8,128)(2,1)}), bf16[16,32,256]{2,1,0:T(8,128)(2,1)S(1)}, u32[]{:S(2)}, u32[]{:S(2)}) %all-to-all-start.2) | async-done | bytes 262176 | tf_op jit(solution)/shard_map/all_to_all | solution.py:287
  63.6 1.4 %shard_map.95 = bf16[16,32,128]{2,1,0:T(8,128)(2,1)} custom-call(bf16[512,256]{1,0:T(8,128)(2,1)S(1)} %bitcast.26, bf16[864,512]{1,0:T(8,128)(2,1)S(1)} %bitcast.27), custom_call_target="tpu_custom_call" | custom-call | flops 226492416 | bytes 1146880 | tf_op jit(solution)/shard_map/pallas_call | solution.py:20
  65.0 4.5 %all-to-all-start.3 = ((bf16[16,32,128]{2,1,0:T(8,128)(2,1)}), bf16[16,32,128]{2,1,0:T(8,128)(2,1)}, u32[]{:S(2)}, u32[]{:S(2)}) async-start(bf16[16,32,128]{2,1,0:T(8,128)(2,1)} %shard_map.95), calls=%async_computation.3 | async-start | bytes 262144 | tf_op jit(solution)/shard_map/all_to_all | solution.py:287
  69.5 1.7 %fusion = bf16[64,8,512]{2,0,1:T(8,128)(2,1)S(1)} fusion(bf16[8,512,256]{2,1,0:T(8,128)(2,1)S(1)} %bitcast.25, bf16[256,256]{1,0:T(8,128)(2,1)} %constant.39.clone.order, s32[]{:T(128)S(6)} %select_n.16), kind=kOutput, calls=%fused_computation | convolution fusion | flops 134217728 | bytes 2686980 | tf_op jit(solution)/shard_map/pio,os->ips/dot_general | solution.py:377
  71.2 0.2 copy.13.rise
  71.4 0.0 copy-start.3
  71.4 5.1 %all-to-all-done.3 = bf16[16,32,128]{2,1,0:T(8,128)(2,1)} async-done(((bf16[16,32,128]{2,1,0:T(8,128)(2,1)}), bf16[16,32,128]{2,1,0:T(8,128)(2,1)}, u32[]{:S(2)}, u32[]{:S(2)}) %all-to-all-start.3) | async-done | bytes 131104 | tf_op jit(solution)/shard_map/all_to_all | solution.py:287
  76.6 1.5 %copy-done.7 = bf16[3,3,3,128,256]{4,3,2,1,0:T(8,128)(2,1)S(1)} copy-done((bf16[3,3,3,128,256]{4,3,2,1,0:T(8,128)(2,1)S(1)}, bf16[3,3,3,128,256]{4,3,2,1,0:T(8,128)(2,1)}, u32[]{:S(2)}) %copy-start.7) | copy-done | bytes 1769496
  78.1 4.0 %shard_map.96 = bf16[512,256]{1,0:T(8,128)(2,1)S(1)} custom-call(s32[1]{0:T(128)} %bitcast.plane, bf16[512,128]{1,0:T(8,128)(2,1)} %bitcast.10.deeper, bf16[512,512]{1,0:T(8,128)(2,1)S(1)} %copy.13.rise, bf16[4,48,256]{2,1,0:T(8,128)(2,1)S(1)} %all-to-all-done.near, bf16[4,80,256]{2,1,0:T(8,128)(2,1)S(1)} %all_to_all.25.pooled.relayed, ...), custom_call_target="tpu_custom_call" | custom-call | flops 905969664 | bytes 2686980 | tf_op jit(solution)/shard_map/pallas_call | solution.py:20
  82.1 8.6 %all_to_all.26.partials = bf16[4,128,256]{2,1,0:T(8,128)(2,1)S(1)} all-to-all(bf16[4,128,256]{2,1,0:T(8,128)(2,1)S(1)} %bitcast.30), channel_id=1, replica_groups={{0,1,2,3},{4,5,6,7},{8,9,10,11},{12,13,14,15},{16,17,18,19},{20,21,22,2..., dimensions={0} | all-to-all | bytes 524288 | tf_op jit(solution)/shard_map/all_to_all | solution.py:287
  90.6 1.1 %shard_map.97 = bf16[1024,128]{1,0:T(8,128)(2,1)} custom-call(bf16[4,128,256]{2,1,0:T(8,128)(2,1)S(1)} %all_to_all.26.partials, bf16[8,256,128]{2,1,0:T(8,128)(2,1)S(1)} %bitcast.28), custom_call_target="tpu_custom_call" | custom-call | flops 67108864 | bytes 786432 | tf_op jit(solution)/shard_map/pallas_call | solution.py:20
  (14 shorter events, 0.0 us)
Async XLA Ops:
  6.5 63.0 %copy-start = (bf16[2,2,2,512,256]{4,3,2,1,0:T(8,128)(2,1)S(1)}, bf16[2,2,2,512,256]{4,3,2,1,0:T(8,128)(2,1)}, u32[]{:S(2)}) copy-start(bf16[2,2,2,512,256]{4,3,2,1,0:T(8,128)(2,1)} %param.14) | copy-start | bytes 6291460
  6.5 70.1 %all-gather.2.cloned.1.call-start = ((), (), s32[]{:S(2)}) async-start(), calls=%async_computation.5 | async-start | bytes 2211840 | tf_op jit(solution)/shard_map/all_gather | solution.py:312
  8.3 10.1 %collective-permute-start = (bf16[3,16,16,128]{3,2,1,0:T(8,128)(2,1)S(1)}, bf16[3,16,16,128]{3,2,1,0:T(8,128)(2,1)S(1)}, u32[]{:S(2)}, u32[]{:S(2)}) collective-permute-start(bf16[3,16,16,128]{3,2,1,0:T(8,128)(2,1)S(1)} %get-tuple-element.6), channel_id=1, source_target_pairs={{0,1},{1,2},{2,3},{3,4},{4,5},{5,6},{6,7},{7,8},{8,9},{9,10},{10,1... | collective-permute-start | bytes 589832 | tf_op jit(solution)/shard_map/ppermute | solution.py:318
  12.9 7.0 %collective-permute-start.1 = (bf16[3,16,16,128]{3,2,1,0:T(8,128)(2,1)S(1)}, bf16[3,16,16,128]{3,2,1,0:T(8,128)(2,1)S(1)}, u32[]{:S(2)}, u32[]{:S(2)}) collective-permute-start(bf16[3,16,16,128]{3,2,1,0:T(8,128)(2,1)S(1)} %get-tuple-element.5), channel_id=1, source_target_pairs={{1,0},{2,1},{3,2},{4,3},{5,4},{6,5},{7,6},{8,7},{9,8},{10,9},{11,1... | collective-permute-start | bytes 589832 | tf_op jit(solution)/shard_map/ppermute | solution.py:319
  14.9 1.0 copy-start.2
  15.8 1.2 %copy-start.8 = (bf16[3,3,3,128,128]{4,3,2,1,0:T(8,128)(2,1)S(1)}, bf16[3,3,3,128,128]{4,3,2,1,0:T(8,128)(2,1)}, u32[]{:S(2)}) copy-start(bf16[3,3,3,128,128]{4,3,2,1,0:T(8,128)(2,1)} %param.10) | copy-start | bytes 2654212
  17.0 2.9 %copy-start.5 = (bf16[256,256]{1,0:T(8,128)(2,1)S(1)}, bf16[256,256]{1,0:T(8,128)(2,1)}, u32[]{:S(2)}) copy-start(bf16[256,256]{1,0:T(8,128)(2,1)} %constant.39.clone.order) | copy-start | bytes 393220
  17.0 2.9 %copy-start.6 = (bf16[3,3,3,128,256]{4,3,2,1,0:T(8,128)(2,1)S(1)}, bf16[3,3,3,128,256]{4,3,2,1,0:T(8,128)(2,1)}, u32[]{:S(2)}) copy-start(bf16[3,3,3,128,256]{4,3,2,1,0:T(8,128)(2,1)} %param.11) | copy-start | bytes 5308420
  17.0 2.9 %copy-start.9 = (bf16[3,3,3,128,128]{4,3,2,1,0:T(8,128)(2,1)S(1)}, bf16[3,3,3,128,128]{4,3,2,1,0:T(8,128)(2,1)}, u32[]{:S(2)}) copy-start(bf16[3,3,3,128,128]{4,3,2,1,0:T(8,128)(2,1)} %param.10) | copy-start | bytes 2654212
  23.4 40.2 %copy-start.1 = (bf16[3,3,3,512,32]{3,4,2,1,0:T(8,128)(2,1)S(1)}, bf16[3,3,3,512,32]{3,4,2,1,0:T(8,128)(2,1)}, u32[]{:S(2)}) copy-start(bf16[3,3,3,512,32]{3,4,2,1,0:T(8,128)(2,1)} %param.13) | copy-start | bytes 2654212
  23.4 7.9 %all-to-all-start = ((bf16[4,48,256]{2,1,0:T(8,128)(2,1)}), bf16[4,48,256]{2,1,0:T(8,128)(2,1)S(1)}, u32[]{:S(2)}, u32[]{:S(2)}) async-start(bf16[4,48,256]{2,1,0:T(8,128)(2,1)} %shard_map.92), calls=%async_computation | async-start | bytes 196608 | tf_op jit(solution)/shard_map/all_to_all | solution.py:287
  46.8 1.0 %copy-start.4 = (bf16[3,3,3,256,32]{3,4,2,1,0:T(8,128)(2,1)S(1)}, bf16[3,3,3,256,32]{3,4,2,1,0:T(8,128)(2,1)}, u32[]{:S(2)}) copy-start(bf16[3,3,3,256,32]{3,4,2,1,0:T(8,128)(2,1)} %param.12) | copy-start | bytes 1327108
  49.1 14.5 %all-to-all-start.2 = ((bf16[16,32,256]{2,1,0:T(8,128)(2,1)}), bf16[16,32,256]{2,1,0:T(8,128)(2,1)S(1)}, u32[]{:S(2)}, u32[]{:S(2)}) async-start(bf16[16,32,256]{2,1,0:T(8,128)(2,1)} %shard_map.94), calls=%async_computation.2 | async-start | bytes 524288 | tf_op jit(solution)/shard_map/all_to_all | solution.py:287
  65.0 11.6 %all-to-all-start.3 = ((bf16[16,32,128]{2,1,0:T(8,128)(2,1)}), bf16[16,32,128]{2,1,0:T(8,128)(2,1)}, u32[]{:S(2)}, u32[]{:S(2)}) async-start(bf16[16,32,128]{2,1,0:T(8,128)(2,1)} %shard_map.95), calls=%async_computation.3 | async-start | bytes 262144 | tf_op jit(solution)/shard_map/all_to_all | solution.py:287
  71.4 19.2 %copy-start.3 = (bf16[2,2,2,256,128]{4,3,2,1,0:T(8,128)(2,1)S(1)}, bf16[2,2,2,256,128]{4,3,2,1,0:T(8,128)(2,1)}, u32[]{:S(2)}) copy-start(bf16[2,2,2,256,128]{4,3,2,1,0:T(8,128)(2,1)} %param.16) | copy-start | bytes 1572868
  76.6 1.5 %copy-start.7 = (bf16[3,3,3,128,256]{4,3,2,1,0:T(8,128)(2,1)S(1)}, bf16[3,3,3,128,256]{4,3,2,1,0:T(8,128)(2,1)}, u32[]{:S(2)}) copy-start(bf16[3,3,3,128,256]{4,3,2,1,0:T(8,128)(2,1)} %all-gather.2.cloned.1.call-done) | copy-start | bytes 5308420
Sparse Core Ops, SparseCore 0:
  8.9 45.8 all-gather.1
